TPU v7x, 32 devices: a whole 2x2x4 slice. The times are simulated.
32 devices in a mesh: dp: 4 (over y, x), gr: 2 (over core), gc: 4 (over z).
Axes of the slice: x: 2, y: 2, z: 4, core: 2. Of those that a mesh axis runs over, the one named last changes fastest.
Arguments:
- frames: float32 [4, 1500, 768], P('dp', 'gc', 'gr'), may hold values from -6 to 6
- cotangent: float32 [4, 1500, 768], P('dp', 'gc', 'gr'), may hold values from -6 to 6
- w_qkv: float32 [768, 3, 768], P('gr', None, 'gc'), may hold values from -0.21875 to 0.21875
- w_out: float32 [768, 768], P('gc', 'gr'), may hold values from -6 to 6
- w_up: float32 [768, 3072], P('gr', 'gc'), may hold values from -0.21875 to 0.21875
- w_down: float32 [3072, 768], P('gc', 'gr'), may hold values from -0.109375 to 0.109375
- vectors: float32 [6, 768], P(None, 'gr'), may hold values from -0.8 to 1.5, as said below
- first_qkv: float32 [768, 3, 768], P(('gr', 'dp'), None, 'gc'), may hold values from -48 to 48
- second_qkv: float32 [768, 3, 768], P(('gr', 'dp'), None, 'gc'), may hold values from 6 to 24
- first_out: float32 [768, 768], P('gc', ('gr', 'dp')), may hold values from -6 to 6
- second_out: float32 [768, 768], P('gc', ('gr', 'dp')), may hold values from 0.015 to 0.06
- first_up: float32 [768, 3072], P(('gr', 'dp'), 'gc'), may hold values from -24 to 24
- second_up: float32 [768, 3072], P(('gr', 'dp'), 'gc'), may hold values from 1.5 to 6
- first_down: float32 [3072, 768], P('gc', ('gr', 'dp')), may hold values from -32 to 32
- second_down: float32 [3072, 768], P('gc', ('gr', 'dp')), may hold values from 2.16 to 8.64
- first_vec: float32 [6, 768], P(None, 'gr'), may hold values from -80 to 80
- second_vec: float32 [6, 768], P(None, 'gr'), may hold values from 13.5 to 54
Outputs:
- block_out: float32 [4, 1500, 768], P('dp', 'gc', 'gr')
- grad_frames: float32 [4, 1500, 768], P('dp', 'gc', 'gr')
- grad_qkv: float32 [768, 3, 768], P(('gr', 'dp'), None, 'gc')
- first_qkv_new: float32 [768, 3, 768], P(('gr', 'dp'), None, 'gc')
- second_qkv_new: float32 [768, 3, 768], P(('gr', 'dp'), None, 'gc')
- w_qkv_new: float32 [768, 3, 768], P(('gr', 'dp'), None, 'gc')
- grad_out: float32 [768, 768], P('gc', ('gr', 'dp'))
- first_out_new: float32 [768, 768], P('gc', ('gr', 'dp'))
- second_out_new: float32 [768, 768], P('gc', ('gr', 'dp'))
- w_out_new: float32 [768, 768], P('gc', ('gr', 'dp'))
- grad_up: float32 [768, 3072], P(('gr', 'dp'), 'gc')
- first_up_new: float32 [768, 3072], P(('gr', 'dp'), 'gc')
- second_up_new: float32 [768, 3072], P(('gr', 'dp'), 'gc')
- w_up_new: float32 [768, 3072], P(('gr', 'dp'), 'gc')
- grad_down: float32 [3072, 768], P('gc', ('gr', 'dp'))
- first_down_new: float32 [3072, 768], P('gc', ('gr', 'dp'))
- second_down_new: float32 [3072, 768], P('gc', ('gr', 'dp'))
- w_down_new: float32 [3072, 768], P('gc', ('gr', 'dp'))
- grad_vectors: float32 [6, 768], P(None, 'gr')
- first_vec_new: float32 [6, 768], P(None, 'gr')
- second_vec_new: float32 [6, 768], P(None, 'gr')
- vectors_new: float32 [6, 768], P(None, 'gr')
Inputs may be any that keep to these rules, and one draw needn't show every extreme that they name: `vectors`: rows 0 and 3 lie in 0.5 to 1.5; the other rows in -0.8 to 0.8.
All inputs are finite; a program needn't handle non-finite values.
Results may differ from a plain program's by a relative error of at most 0.00018.
Values sent between devices are 32-bit elements; how exact they have to be, the bound alone decides.
A program may use at most 128 MiB of HBM per device.

v0:
```python
import jax
import jax.numpy as jnp
from jax import lax
from jax.sharding import PartitionSpec as P

HD = 64
STEP = 10


norm_eps = 1e-05
learn_rate = 0.1
beta_first = 0.9
beta_second = 0.999
adam_epsilon = 1e-08
weight_decay = 0.01
highest = lax.Precision.HIGHEST


def width_sums(first_part, second_part):
    return lax.psum((first_part, second_part), "gr")


def token_rows(pieces):
    return lax.all_gather(pieces, "gc", axis=1, tiled=True)


def partial_width(partial_value):
    return lax.psum_scatter(partial_value, "gr", scatter_dimension=1, tiled=True)


def half_rows(pieces):
    return lax.all_gather(pieces, "gr", axis=1, tiled=True)


def partial_heads(partial_value):
    return lax.psum_scatter(partial_value, "gc", scatter_dimension=1, tiled=True)


def gelu_exact(inputs):
    return jax.nn.gelu(inputs, approximate=False)


def norm_forward(inputs, norm_gain, norm_bias):
    entries = inputs.shape[-1] * lax.axis_size("gr")
    totals, squares = width_sums(
        jnp.sum(inputs, -1, keepdims=True), jnp.sum(inputs * inputs, -1, keepdims=True)
    )
    average = totals / entries
    row_scale = lax.rsqrt(squares / entries - average * average + norm_eps)
    normalized = (inputs - average) * row_scale
    return (normalized * norm_gain + norm_bias, normalized, row_scale)


def norm_backward(grad_normed, normalized, row_scale, norm_gain):
    entries = normalized.shape[-1] * lax.axis_size("gr")
    grad_unit = grad_normed * norm_gain
    totals, crossed = width_sums(
        jnp.sum(grad_unit, -1, keepdims=True), jnp.sum(grad_unit * normalized, -1, keepdims=True)
    )
    grad_inputs = row_scale * (grad_unit - totals / entries - normalized * (crossed / entries))
    return (grad_inputs, jnp.sum(grad_normed * normalized, (0, 1)), jnp.sum(grad_normed, (0, 1)))


def attend_forward(inputs):
    queries, key_block, value_block = inputs
    scores = jnp.einsum("qhe,khe->hqk", queries, key_block, precision=highest) * HD ** (-0.5)
    top_score = jnp.max(scores, -1, keepdims=True)
    weights = jnp.exp(scores - top_score)
    totals = jnp.sum(weights, -1, keepdims=True)
    attended = jnp.einsum("hqk,khe->qhe", weights / totals, value_block, precision=highest)
    return (attended, (top_score + jnp.log(totals))[:, :, 0])


def attend_backward(inputs):
    queries, key_block, value_block, attended, log_total, grad_attended = inputs
    scores = jnp.einsum("qhe,khe->hqk", queries, key_block, precision=highest) * HD ** (-0.5)
    weights = jnp.exp(scores - log_total[:, :, None])
    grad_values = jnp.einsum("hqk,qhe->khe", weights, grad_attended, precision=highest)
    grad_weights = jnp.einsum("qhe,khe->hqk", grad_attended, value_block, precision=highest)
    row_dots = jnp.transpose(jnp.sum(grad_attended * attended, -1))
    grad_scores = weights * (grad_weights - row_dots[:, :, None]) * HD ** (-0.5)
    grad_queries = jnp.einsum("hqk,khe->qhe", grad_scores, key_block, precision=highest)
    grad_keys = jnp.einsum("hqk,qhe->khe", grad_scores, queries, precision=highest)
    return (grad_queries, grad_keys, grad_values)


def owned_block(weight_block, dim_index, owned_count):
    return lax.dynamic_slice_in_dim(
        weight_block, lax.axis_index("dp") * owned_count, owned_count, dim_index
    )


def adamw(weight_old, gradient, first_old, second_old, decay_rate):
    first_new = beta_first * first_old + (1.0 - beta_first) * gradient
    second_new = beta_second * second_old + (1.0 - beta_second) * gradient * gradient
    step_dir = (
        first_new
        / (1.0 - beta_first**STEP)
        / (jnp.sqrt(second_new / (1.0 - beta_second**STEP)) + adam_epsilon)
    )
    return (first_new, second_new, weight_old - learn_rate * (step_dir + decay_rate * weight_old))


def local(
    frames,
    cotangent,
    w_qkv,
    w_out,
    w_up,
    w_down,
    vectors,
    first_qkv,
    second_qkv,
    first_out,
    second_out,
    first_up,
    second_up,
    first_down,
    second_down,
    first_vec,
    second_vec,
):
    clip_count = frames.shape[0]
    local_heads = w_qkv.shape[2] // HD
    normed, unit_one, scale_one = norm_forward(frames, vectors[0], vectors[1])
    normed_all = token_rows(normed)
    mixed_qkv = partial_width(jnp.einsum("bld,djn->bljn", normed_all, w_qkv, precision=highest))
    half_len = mixed_qkv.shape[1]
    split_qkv = mixed_qkv.reshape(clip_count, half_len, 3, local_heads, HD)
    queries = split_qkv[:, :, 0]
    keys_all, values_all = (
        lax.all_gather(split_qkv[:, :, 1], "gr", axis=1, tiled=True),
        lax.all_gather(split_qkv[:, :, 2], "gr", axis=1, tiled=True),
    )
    attended, log_total = lax.map(attend_forward, (queries, keys_all, values_all))
    attn_all = half_rows(attended.reshape(clip_count, half_len, local_heads * HD))
    middle = (
        frames
        + partial_heads(jnp.einsum("bln,nd->bld", attn_all, w_out, precision=highest))
        + vectors[2]
    )
    normed_two, unit_two, scale_two = norm_forward(middle, vectors[3], vectors[4])
    normed_two_all = token_rows(normed_two)
    hidden = partial_width(jnp.einsum("bld,df->blf", normed_two_all, w_up, precision=highest))
    active, gelu_pull = jax.vjp(gelu_exact, hidden)
    active_all = half_rows(active)
    block_out = (
        middle
        + partial_heads(jnp.einsum("blf,fd->bld", active_all, w_down, precision=highest))
        + vectors[5]
    )
    grad_all = token_rows(cotangent)
    grad_down = jnp.einsum("blf,bld->fd", active_all, grad_all, precision=highest)
    grad_active = partial_width(jnp.einsum("bld,fd->blf", grad_all, w_down, precision=highest))
    grad_hidden = gelu_pull(grad_active)[0]
    grad_hidden_all = half_rows(grad_hidden)
    grad_up = jnp.einsum("bld,blf->df", normed_two_all, grad_hidden_all, precision=highest)
    grad_normed_two = partial_heads(
        jnp.einsum("blf,df->bld", grad_hidden_all, w_up, precision=highest)
    )
    grad_middle_norm, grad_gain_two, grad_bias_two = norm_backward(
        grad_normed_two, unit_two, scale_two, vectors[3]
    )
    grad_middle = cotangent + grad_middle_norm
    grad_middle_all = token_rows(grad_middle)
    grad_out = jnp.einsum("bln,bld->nd", attn_all, grad_middle_all, precision=highest)
    grad_attn = partial_width(jnp.einsum("bld,nd->bln", grad_middle_all, w_out, precision=highest))
    grad_attn = grad_attn.reshape(clip_count, half_len, local_heads, HD)
    grad_queries, grad_key_part, grad_value_part = lax.map(
        attend_backward, (queries, keys_all, values_all, attended, log_total, grad_attn)
    )
    grad_keys, grad_values = (
        lax.psum_scatter(grad_key_part, "gr", scatter_dimension=1, tiled=True),
        lax.psum_scatter(grad_value_part, "gr", scatter_dimension=1, tiled=True),
    )
    grad_mixed = jnp.stack((grad_queries, grad_keys, grad_values), 2).reshape(
        clip_count, half_len, 3, local_heads * HD
    )
    grad_mixed_all = half_rows(grad_mixed)
    grad_qkv = jnp.einsum("bld,bljn->djn", normed_all, grad_mixed_all, precision=highest)
    grad_normed = partial_heads(
        jnp.einsum("bljn,djn->bld", grad_mixed_all, w_qkv, precision=highest)
    )
    grad_inputs, grad_gain_one, grad_bias_one = norm_backward(
        grad_normed, unit_one, scale_one, vectors[0]
    )
    grad_frames = grad_middle + grad_inputs
    vector_local = jnp.stack(
        (
            grad_gain_one,
            grad_bias_one,
            jnp.sum(grad_middle, (0, 1)),
            grad_gain_two,
            grad_bias_two,
            jnp.sum(cotangent, (0, 1)),
        )
    )
    grad_vectors = lax.psum(vector_local, ("dp", "gc"))
    grad_qkv, grad_out, grad_up, grad_down = (
        lax.psum_scatter(grad_qkv, "dp", scatter_dimension=0, tiled=True),
        lax.psum_scatter(grad_out, "dp", scatter_dimension=1, tiled=True),
        lax.psum_scatter(grad_up, "dp", scatter_dimension=0, tiled=True),
        lax.psum_scatter(grad_down, "dp", scatter_dimension=1, tiled=True),
    )
    first_qkv_new, second_qkv_new, w_qkv_new = adamw(
        owned_block(w_qkv, 0, grad_qkv.shape[0]), grad_qkv, first_qkv, second_qkv, weight_decay
    )
    first_out_new, second_out_new, w_out_new = adamw(
        owned_block(w_out, 1, grad_out.shape[1]), grad_out, first_out, second_out, weight_decay
    )
    first_up_new, second_up_new, w_up_new = adamw(
        owned_block(w_up, 0, grad_up.shape[0]), grad_up, first_up, second_up, weight_decay
    )
    first_down_new, second_down_new, w_down_new = adamw(
        owned_block(w_down, 1, grad_down.shape[1]), grad_down, first_down, second_down, weight_decay
    )
    first_vec_new, second_vec_new, vectors_new = adamw(
        vectors, grad_vectors, first_vec, second_vec, 0.0
    )
    return (
        block_out,
        grad_frames,
        grad_qkv,
        first_qkv_new,
        second_qkv_new,
        w_qkv_new,
        grad_out,
        first_out_new,
        second_out_new,
        w_out_new,
        grad_up,
        first_up_new,
        second_up_new,
        w_up_new,
        grad_down,
        first_down_new,
        second_down_new,
        w_down_new,
        grad_vectors,
        first_vec_new,
        second_vec_new,
        vectors_new,
    )


def solution(mesh):
    return jax.shard_map(
        local,
        mesh=mesh,
        in_specs=(
            P("dp", "gc", "gr"),
            P("dp", "gc", "gr"),
            P("gr", None, "gc"),
            P("gc", "gr"),
            P("gr", "gc"),
            P("gc", "gr"),
            P(None, "gr"),
            P(("gr", "dp"), None, "gc"),
            P(("gr", "dp"), None, "gc"),
            P("gc", ("gr", "dp")),
            P("gc", ("gr", "dp")),
            P(("gr", "dp"), "gc"),
            P(("gr", "dp"), "gc"),
            P("gc", ("gr", "dp")),
            P("gc", ("gr", "dp")),
            P(None, "gr"),
            P(None, "gr"),
        ),
        out_specs=(
            P("dp", "gc", "gr"),
            P("dp", "gc", "gr"),
            P(("gr", "dp"), None, "gc"),
            P(("gr", "dp"), None, "gc"),
            P(("gr", "dp"), None, "gc"),
            P(("gr", "dp"), None, "gc"),
            P("gc", ("gr", "dp")),
            P("gc", ("gr", "dp")),
            P("gc", ("gr", "dp")),
            P("gc", ("gr", "dp")),
            P(("gr", "dp"), "gc"),
            P(("gr", "dp"), "gc"),
            P(("gr", "dp"), "gc"),
            P(("gr", "dp"), "gc"),
            P("gc", ("gr", "dp")),
            P("gc", ("gr", "dp")),
            P("gc", ("gr", "dp")),
            P("gc", ("gr", "dp")),
            P(None, "gr"),
            P(None, "gr"),
            P(None, "gr"),
            P(None, "gr"),
        ),
        check_vma=False,
    )
```

profile of v0, /device:TPU:0, one launch (start us, length us, event | category | flops | bytes accessed | tf_op | source)
XLA Modules:
  0.0 1229.8 jit_solution(5961265028290300294)
XLA Ops:
  17.7 52.3 %all-gather.13.cloned.1.call-done = f32[1,1500,384]{2,0,1:T(1,128)} async-done(((f32[1,375,384]{2,0,1:T(1,128)}), f32[1,1500,384]{2,0,1:T(1,128)}) %all-gather.13.cloned.1.call-update) | async-done | bytes 2304016 | tf_op jit(solution)/shard_map/all_gather | solution.py:24
  80.4 21.1 %all-reduce.25.cloned.1.call-done = f32[1,1500,3,192]{1,3,2,0:T(8,128)} async-done(((f32[1,1500,3,192]{1,3,2,0:T(8,128)}), f32[1,1500,3,192]{1,3,2,0:T(8,128)}) %all-reduce.25.cloned.1.call-update) | async-done | bytes 3456016
  125.2 15.0 %multiply_reduce_fusion = (f32[3,750]{1,0:T(4,128)S(1)}, f32[3,750,1500]{2,1,0:T(8,128)}) fusion(f32[1,1500,1,3,64]{1,4,3,2,0:T(8,128)S(1)} %copy.73, f32[1,750,3,3,64]{1,4,3,2,0:T(8,128)} %bitcast.143), kind=kOutput, calls=%fused_computation.9 | convolution fusion | flops 2598747648 | bytes 15250824 | tf_op jit(solution)/shard_map/while/body/eval_jaxpr/qhe,khe->hqk/dot_general | solution.py:66
  153.6 19.0 %fusion = f32[3,64,750]{2,1,0:T(8,128)} fusion(f32[3,750,1500]{2,1,0:T(8,128)} %get-tuple-element.178, f32[3,750]{1,0:T(4,128)} %fusion.2, f32[3,750]{1,0:T(4,128)S(1)} %get-tuple-element.177, f32[1,1500,1,3,64]{1,4,3,2,0:T(8,128)S(1)} %copy.71), kind=kOutput, calls=%fused_computation.3 | convolution fusion | flops 2602125056 | bytes 15246000 | tf_op jit(solution)/shard_map/while/body/eval_jaxpr/hqk,khe->qhe/dot_general | solution.py:70
  204.6 92.8 %all-reduce.27.cloned.1.call-done = f32[1,1500,384]{2,0,1:T(1,128)} async-done(((f32[1,1500,384]{2,0,1:T(1,128)}), f32[1,1500,384]{2,0,1:T(1,128)}) %all-reduce.27.cloned.1.call-update) | async-done | bytes 2304016
  305.5 42.2 %all-gather.21.cloned.1.call-done = f32[1,1500,384]{2,0,1:T(1,128)} async-done(((f32[1,375,384]{2,0,1:T(1,128)}), f32[1,1500,384]{2,0,1:T(1,128)}) %all-gather.21.cloned.1.call-update) | async-done | bytes 2304016 | tf_op jit(solution)/shard_map/all_gather | solution.py:24
  358.2 26.0 %copy.79 = f32[1,1500,768]{2,0,1:T(1,128)} copy(f32[1,1500,768]{2,1,0:T(8,128)S(1)} %convolution_bitcast_fusion) | data formatting | bytes 9216000 | tf_op jit(solution)/shard_map/bld,fd->blf/dot_general | solution.py:154
  384.2 13.5 %all-gather.17.cloned.1.call-done = f32[1,1500,384]{2,0,1:T(1,128)} async-done(((f32[1,375,384]{2,0,1:T(1,128)}), f32[1,1500,384]{2,0,1:T(1,128)}) %all-gather.17.cloned.1.call-update) | async-done | bytes 2304016 | tf_op jit(solution)/shard_map/all_gather | solution.py:24
  408.1 26.0 %copy.77 = f32[1,1500,768]{2,0,1:T(1,128)} copy(f32[1,1500,768]{2,1,0:T(8,128)S(1)} %convolution_bitcast_fusion.1) | data formatting | bytes 9216000 | tf_op jit(solution)/shard_map/bld,df->blf/dot_general | solution.py:144
  434.2 39.3 %all-reduce.37.cloned.1.call-done = (f32[1,1500,768]{2,0,1:T(1,128)}, f32[1,1500,768]{2,0,1:T(1,128)}) async-done(((f32[1,1500,768]{2,0,1:T(1,128)}, f32[1,1500,768]{2,0,1:T(1,128)}), (f32[1,1500,768]{2,0,1:T(1,128)}, f32[1,1500,768]{2,0,1:T(1,128)})) %all-reduce.37.cloned.1.call-update) | async-done | bytes 9216016
  473.5 44.8 %multiply_add_fusion = (f32[1,750,768]{2,0,1:T(1,128)}, f32[1,750,768]{2,0,1:T(1,128)}) fusion(f32[1,1500,768]{2,0,1:T(1,128)} %get-tuple-element.149, u32[]{:T(128)S(6)} %multiply.19, f32[1,1500,768]{2,0,1:T(1,128)} %get-tuple-element.148), kind=kLoop, calls=%fused_computation.57 | loop fusion | flops 40896000 | bytes 9216004 | tf_op jit(solution)/shard_map/transpose(jvp())/add_any | solution.py:40
  518.3 15.6 %all-gather.23.cloned.1.call-done = f32[1,1500,768]{2,0,1:T(1,128)} async-done(((f32[1,750,768]{2,0,1:T(1,128)}), f32[1,1500,768]{2,0,1:T(1,128)}) %all-gather.23.cloned.1.call-update) | async-done | bytes 4608016 | tf_op jit(solution)/shard_map/all_gather | solution.py:32
  551.6 95.0 %all-reduce.29.cloned.1.call-done = f32[1,1500,384]{2,0,1:T(1,128)} async-done(((f32[1,1500,384]{2,0,1:T(1,128)}), f32[1,1500,384]{2,0,1:T(1,128)}) %all-reduce.29.cloned.1.call-update) | async-done | bytes 2304016
  659.3 48.8 %all-gather.25.cloned.1.call-done = f32[1,1500,384]{2,0,1:T(1,128)} async-done(((f32[1,375,384]{2,0,1:T(1,128)}), f32[1,1500,384]{2,0,1:T(1,128)}) %all-gather.25.cloned.1.call-update) | async-done | bytes 2304016 | tf_op jit(solution)/shard_map/all_gather | solution.py:24
  714.0 18.3 %all-reduce.31.cloned.1.call-done = f32[1,1500,192]{1,2,0:T(8,128)} async-done(((f32[1,1500,192]{1,2,0:T(8,128)}), f32[1,1500,192]{1,2,0:T(8,128)}) %all-reduce.31.cloned.1.call-update) | async-done | bytes 1152016
  733.7 14.2 %fusion.36 = f32[1,1500,3,64]{1,3,2,0:T(8,128)} fusion(f32[750,3,64]{0,2,1:T(8,128)S(1)} %bitcast.146, f32[3,750,1500]{2,1,0:T(8,128)} %get-tuple-element.178, f32[3,750]{1,0:T(4,128)S(1)} %log_add_fusion), kind=kOutput, calls=%fused_computation.42 | convolution fusion | flops 2598749952 | bytes 15237000 | tf_op jit(solution)/shard_map/while/body/eval_jaxpr/hqk,qhe->khe/dot_general | solution.py:78
  747.9 16.8 %multiply_multiply_fusion = f32[3,750,1500]{2,1,0:T(8,128)S(1)} fusion(f32[3,750,1500]{2,1,0:T(8,128)} %get-tuple-element.178, f32[750,3,64]{0,2,1:T(8,128)S(1)} %bitcast.147, f32[3,750]{1,0:T(4,128)S(1)} %bitcast.154, f32[3,750]{1,0:T(4,128)S(1)} %log_add_fusion, f32[1,1500,1,3,64]{1,4,3,2,0:T(8,128)S(1)} %copy-done.18), kind=kOutput, calls=%fused_computation | convolution fusion | flops 2608875008 | bytes 28746000 | tf_op jit(solution)/shard_map/while/body/eval_jaxpr/qhe,khe->hqk/dot_general | solution.py:79
  787.3 15.7 %fusion.62 = f32[3,64,750]{2,1,0:T(8,128)S(1)} fusion(f32[3,750,1500]{2,1,0:T(8,128)} %copy-done.1, f32[1,1500,1,3,64]{1,4,3,2,0:T(8,128)S(1)} %copy.73), kind=kOutput, calls=%fused_computation.73 | convolution fusion | flops 2592000000 | bytes 15228000 | tf_op jit(solution)/shard_map/while/body/eval_jaxpr/hqk,khe->qhe/dot_general | solution.py:82
  843.1 12.1 copy.84
  855.2 14.2 %fusion.23 = f32[384,3,192]{2,0,1:T(8,128)} fusion(f32[1,1500,3,192]{1,3,2,0:T(8,128)} %copy.84, f32[1,1500,384]{2,0,1:T(1,128)S(1)} %copy-done.7), kind=kOutput, calls=%fused_computation.33 | convolution fusion | flops 3981312000 | bytes 6644736 | tf_op jit(solution)/shard_map/bld,bljn->djn/dot_general | solution.py:180
  909.0 21.2 %reduce-scatter.17.cloned.1.call-done = f32[96,192]{1,0:T(8,128)} async-done(((f32[384,192]{1,0:T(8,128)}), f32[96,192]{1,0:T(8,128)}) %reduce-scatter.17.cloned.1.call-update) | async-done | bytes 73744
  933.0 29.4 %reduce-scatter.11.cloned.1.call-done = f32[96,3,192]{2,0,1:T(8,128)} async-done(((f32[384,3,192]{2,0,1:T(8,128)}), f32[96,3,192]{2,0,1:T(8,128)}) %reduce-scatter.11.cloned.1.call-update) | async-done | bytes 221200 | tf_op jit(solution)/shard_map/reduce_scatter | solution.py:200
  964.6 169.3 %all-reduce.33.cloned.1.call-done = (f32[1,1500,384]{2,0,1:T(1,128)}, f32[1,1500,384]{2,0,1:T(1,128)}) async-done(((f32[1,1500,384]{2,0,1:T(1,128)}, f32[1,1500,384]{2,0,1:T(1,128)}), (f32[1,1500,384]{2,0,1:T(1,128)}, f32[1,1500,384]{2,0,1:T(1,128)})) %all-reduce.33.cloned.1.call-update) | async-done | bytes 4608016
  1140.3 75.0 %psum.71 = f32[6,384]{1,0:T(8,128)S(1)} all-reduce(f32[6,384]{1,0:T(8,128)S(1)} %stack.43), channel_id=1, replica_groups=mesh['dp'=4,'gr'=2,'gc'=4] {'dp','gc'}, use_global_device_ids=true, to_apply=%region_39.40 | all-reduce | flops 2304 | bytes 18432 | tf_op jit(solution)/shard_map/psum | solution.py:198
  (215 shorter events, 275.3 us)
Async XLA Ops:
  7.2 340.6 %copy-start = (f32[768,384]{1,0:T(8,128)S(1)}, f32[768,384]{1,0:T(8,128)}, u32[]{:S(2)}) copy-start(f32[768,384]{1,0:T(8,128)} %param.22) | copy-start | bytes 3538948
  7.2 62.7 %all-gather.13.cloned.1.call-start = ((), (), s32[]{:S(2)}) async-start(), calls=%async_computation.4 | async-start | bytes 2880000 | tf_op jit(solution)/shard_map/all_gather | solution.py:24
  17.6 83.8 %all-reduce.25.cloned.1.call-start = ((), (), s32[]{:S(2)}) async-start(), calls=%async_computation.18 | async-start | bytes 7077888
  78.6 41.2 %all-gather.31.cloned.1.call-start = ((), (), s32[]{:S(2)}) async-start(), calls=%async_computation.16 | async-start | bytes 3456000 | tf_op jit(solution)/shard_map/all_gather | solution.py:132
  107.5 40.6 %all-gather.29.cloned.1.call-start = ((), (), s32[]{:S(2)}) async-start(), calls=%async_computation.15 | async-start | bytes 3456000 | tf_op jit(solution)/shard_map/all_gather | solution.py:133
  110.2 76.5 %all-gather.15.cloned.1.call-start = ((), (), s32[]{:S(2)}) async-start(), calls=%async_computation.5 | async-start | bytes 2304000 | tf_op jit(solution)/shard_map/all_gather | solution.py:32
  175.6 121.8 %all-reduce.27.cloned.1.call-start = ((), (), s32[]{:S(2)}) async-start(), calls=%async_computation.19 | async-start | bytes 4608000
  202.1 145.6 %all-gather.21.cloned.1.call-start = ((), (), s32[]{:S(2)}) async-start(), calls=%async_computation.8 | async-start | bytes 2880000 | tf_op jit(solution)/shard_map/all_gather | solution.py:24
  202.8 194.9 %all-gather.17.cloned.1.call-start = ((), (), s32[]{:S(2)}) async-start(), calls=%async_computation.6 | async-start | bytes 2880000 | tf_op jit(solution)/shard_map/all_gather | solution.py:24
  305.4 168.0 %all-reduce.37.cloned.1.call-start = ((), (), s32[]{:S(2)}) async-start(), calls=%async_computation.24 | async-start | bytes 18432000
  434.1 99.8 %all-gather.23.cloned.1.call-start = ((), (), s32[]{:S(2)}) async-start(), calls=%async_computation.9 | async-start | bytes 6912000 | tf_op jit(solution)/shard_map/all_gather | solution.py:32
  518.3 128.4 %all-reduce.29.cloned.1.call-start = ((), (), s32[]{:S(2)}) async-start(), calls=%async_computation.20 | async-start | bytes 4608000
  551.3 156.7 %all-gather.25.cloned.1.call-start = ((), (), s32[]{:S(2)}) async-start(), calls=%async_computation.10 | async-start | bytes 2880000 | tf_op jit(solution)/shard_map/all_gather | solution.py:24
  659.2 73.0 %all-reduce.31.cloned.1.call-start = ((), (), s32[]{:S(2)}) async-start(), calls=%async_computation.21 | async-start | bytes 2359296
  713.5 90.7 %all-reduce.35.cloned.1.call-start = ((), (), s32[]{:S(2)}) async-start(), calls=%async_computation.23 | async-start | bytes 4718592
  780.3 45.8 %all-gather.19.cloned.1.call-start = ((), (), s32[]{:S(2)}) async-start(), calls=%async_computation.7 | async-start | bytes 6912000 | tf_op jit(solution)/shard_map/all_gather | solution.py:32
  787.3 55.8 %all-gather.27.cloned.1.call-start = ((), (), s32[]{:S(2)}) async-start(), calls=%async_computation.11 | async-start | bytes 6912000 | tf_op jit(solution)/shard_map/all_gather | solution.py:32
  814.0 90.4 %reduce-scatter.13.cloned.1.call-start = ((), (), s32[]{:S(2)}) async-start(), calls=%async_computation.13 | async-start | bytes 1474560 | tf_op jit(solution)/shard_map/reduce_scatter | solution.py:202
  826.0 80.7 %reduce-scatter.15.cloned.1.call-start = ((), (), s32[]{:S(2)}) async-start(), calls=%async_computation.14 | async-start | bytes 1474560 | tf_op jit(solution)/shard_map/reduce_scatter | solution.py:203
  836.5 93.7 %reduce-scatter.17.cloned.1.call-start = ((), (), s32[]{:S(2)}) async-start(), calls=%async_computation.17 | async-start | bytes 491520
  842.8 119.5 %reduce-scatter.11.cloned.1.call-start = ((), (), s32[]{:S(2)}) async-start(), calls=%async_computation.12 | async-start | bytes 1474560 | tf_op jit(solution)/shard_map/reduce_scatter | solution.py:200
  869.4 264.4 %all-reduce.33.cloned.1.call-start = ((), (), s32[]{:S(2)}) async-start(), calls=%async_computation.22 | async-start | bytes 9216000
  909.0 306.3 %copy-start.14 = (f32[1,375,384]{2,0,1:T(1,128)S(1)}, f32[1,375,384]{2,0,1:T(1,128)}, u32[]{:S(2)}) copy-start(f32[1,375,384]{2,0,1:T(1,128)} %copy-done.13) | copy-start | bytes 1728004
  909.0 306.3 %copy-start.37 = (f32[384]{0:T(512)S(1)}, f32[384]{0:T(512)}, u32[]{:S(2)}) copy-start(f32[384]{0:T(512)} %get-tuple-element.126) | copy-start | bytes 4612
  (39 other events, 2671.7 us)
Sparse Core Ops, SparseCore 0:
  17.8 52.1 all-gather.12
  78.7 22.7 all-reduce.24
  107.7 12.0 all-gather.30
  121.2 12.0 all-gather.28
  175.7 10.8 all-gather.14
  202.2 95.1 all-reduce.26
  299.0 48.6 all-gather.20
  349.3 48.3 all-gather.16
  434.2 39.1 all-reduce.36
  518.4 15.5 all-gather.22
  551.5 95.1 all-reduce.28
  659.3 48.6 all-gather.24
  713.6 18.6 all-reduce.30
  780.4 22.8 all-reduce.34
  804.8 15.4 all-gather.18
  821.7 15.4 all-gather.26
  840.8 29.7 reduce-scatter.12
  874.2 28.5 reduce-scatter.14
  905.8 24.4 reduce-scatter.16
  933.8 28.5 reduce-scatter.10
  965.0 168.8 all-reduce.32
where the time goes:
time: 1240 us; the launch traced here: 1230 us
  waiting for transfers between devices  680 us (55%)
  matrix products  198 us (16%)
  local copies, waits for them, and re-layouts  143 us (12%)
  other arithmetic  103 us (8%)
  blocking collectives  85.6 us (7%)
  between operations  16.8 us (1%)
    unnamed x29, waiting for transfers between devices  458 us
    all_gather x4, waiting for transfers between devices, token_rows(): return lax.all_gather(pieces, 'gc', axis=1, tiled=True)  157 us
    psum x1, blocking collectives, local(): grad_vectors = lax.psum(vector_local, ('dp', 'gc'))  75 us
    add_any x1, other arithmetic, gelu_exact(): return jax.nn.gelu(inputs, approximate=False)  44.8 us
    reduce_scatter x1, waiting for transfers between devices, local(): lax.psum_scatter(grad_qkv, 'dp', scatter_dimension=0, tiled=True)  29.4 us
    all_gather x4, waiting for transfers between devices, half_rows(): return lax.all_gather(pieces, 'gr', axis=1, tiled=True)  26.7 us
    dot_general x1, local copies, waits for them, and re-layouts, local(): jnp.einsum('bld,fd->blf', grad_all, w_down, precision=highest)  26 us
    dot_general x1, local copies, waits for them, and re-layouts, local(): jnp.einsum('bld,df->blf', normed_two_all, w_up, precision=highest)  26 us
  transfers between devices with their start and end apart: 21, of which 15 were waited for; matrix products, arithmetic and copies ran while one was open for 17% of the time, Pallas kernels for 0%

commit v1 on v0

v1 whole, which is shorter than its diff:
```python
import functools

import jax
import jax.numpy as jnp
from jax import lax
from jax.experimental import pallas as pl
from jax.experimental.pallas import tpu as pltpu
from jax.sharding import PartitionSpec as P

HD = 64
STEP = 10


norm_eps = 1e-05
learn_rate = 0.1
beta_first = 0.9
beta_second = 0.999
adam_epsilon = 1e-08
weight_decay = 0.01
high = lax.Precision.HIGH
swap_pairs = ((0, 1), (1, 0))
row_tile = 64
masked = -1e30


def product(spec, left, right):
    return jnp.einsum(spec, left, right, precision=high)


def gather_tokens(rows):
    return lax.all_gather(rows, "gc", axis=0, tiled=True)


def scatter_tokens(partial_value):
    return lax.psum_scatter(partial_value, "gc", scatter_dimension=0, tiled=True)


def other_core(value):
    return lax.ppermute(value, "gr", swap_pairs)


def in_core_order(mine, theirs, axis):
    first = lax.axis_index("gr") == 0
    return jnp.concatenate((jnp.where(first, mine, theirs), jnp.where(first, theirs, mine)), axis)


def own_rows(piece, row_count):
    padded = jnp.pad(piece, ((0, 2 * row_count - piece.shape[0]), (0, 0)))
    core = lax.axis_index("gr")
    mine = lax.dynamic_slice_in_dim(padded, core * row_count, row_count, 0)
    sent = lax.dynamic_slice_in_dim(padded, (1 - core) * row_count, row_count, 0)
    return in_core_order(mine, other_core(sent), 1)


def own_width(rows, frame_count):
    half = rows.shape[1] // 2
    core = lax.axis_index("gr")
    mine = lax.dynamic_slice_in_dim(rows, core * half, half, 1)
    sent = lax.dynamic_slice_in_dim(rows, (1 - core) * half, half, 1)
    return in_core_order(mine, other_core(sent), 0)[:frame_count]


def own_half_sum(partial_value):
    half = partial_value.shape[0] // 2
    core = lax.axis_index("gr")
    mine = lax.dynamic_slice_in_dim(partial_value, core * half, half, 0)
    sent = lax.dynamic_slice_in_dim(partial_value, (1 - core) * half, half, 0)
    return mine + other_core(sent)


def norm_forward(inputs, norm_gain, norm_bias):
    average = jnp.mean(inputs, -1, keepdims=True)
    centred = inputs - average
    row_scale = lax.rsqrt(jnp.mean(centred * centred, -1, keepdims=True) + norm_eps)
    normalized = centred * row_scale
    return (normalized * norm_gain + norm_bias, normalized, row_scale)


def norm_backward(grad_normed, normalized, row_scale, norm_gain):
    grad_unit = grad_normed * norm_gain
    grad_inputs = row_scale * (
        grad_unit
        - jnp.mean(grad_unit, -1, keepdims=True)
        - normalized * jnp.mean(grad_unit * normalized, -1, keepdims=True)
    )
    return (grad_inputs, jnp.sum(grad_normed * normalized, 0), jnp.sum(grad_normed, 0))


def split_parts(value):
    upper = value.astype(jnp.bfloat16)
    return upper, (value - upper.astype(jnp.float32)).astype(jnp.bfloat16)


def left_three(value):
    upper, lower = split_parts(value)
    return jnp.concatenate((upper, upper, lower), -1)


def right_three(value):
    upper, lower = split_parts(value)
    return jnp.concatenate((upper, lower, upper), -1)


def dot_rows(left, right):
    return lax.dot_general(left, right, (((1,), (1,)), ((), ())), preferred_element_type=jnp.float32)


def dot_plain(left, right):
    return jnp.dot(left, right, preferred_element_type=jnp.float32)


def attend_kernel(heads, q_ref, k_ref, vt_ref, mask_ref, out_ref, lse_ref, k_three, vt_two):
    @pl.when(pl.program_id(0) == 0)
    def _():
        for head in range(heads):
            cols = slice(head * HD, (head + 1) * HD)
            k_three[head] = left_three(k_ref[:, cols])
            vt_two[head] = jnp.concatenate(split_parts(vt_ref[cols, :]), 0)

    for head in range(heads):
        cols = slice(head * HD, (head + 1) * HD)
        q_three = right_three(q_ref[:, cols] * HD ** (-0.5))
        scores = dot_rows(k_three[head], q_three) + mask_ref[...]
        top = jnp.max(scores, 0, keepdims=True)
        weights = jnp.exp(scores - top)
        totals = jnp.sum(weights, 0, keepdims=True)
        upper, lower = split_parts(weights)
        both = dot_plain(vt_two[head], upper)
        summed = both[:HD] + both[HD:] + dot_plain(vt_two[head, :HD], lower)
        out_ref[cols, :] = summed / totals
        lse_ref[head : head + 1, :] = top + jnp.log(totals)


def attend_back_kernel(
    heads, q_ref, k_ref, v_ref, kt_ref, mask_ref, lse_ref, delta_ref, do_ref,
    dq_ref, dk_ref, dv_ref, k_three, v_three, kt_two,
):
    @pl.when(pl.program_id(0) == 0)
    def _():
        for head in range(heads):
            cols = slice(head * HD, (head + 1) * HD)
            k_three[head] = left_three(k_ref[:, cols])
            v_three[head] = left_three(v_ref[:, cols])
            kt_two[head] = jnp.concatenate(split_parts(kt_ref[cols, :]), 0)
        dk_ref[...] = jnp.zeros_like(dk_ref)
        dv_ref[...] = jnp.zeros_like(dv_ref)

    for head in range(heads):
        cols = slice(head * HD, (head + 1) * HD)
        q_up, q_low = split_parts(q_ref[:, cols] * HD ** (-0.5))
        do_up, do_low = split_parts(do_ref[:, cols])
        scores = dot_rows(k_three[head], jnp.concatenate((q_up, q_low, q_up), -1)) + mask_ref[...]
        weights = jnp.exp(scores - lse_ref[head : head + 1, :])
        grad_weights = dot_rows(v_three[head], jnp.concatenate((do_up, do_low, do_up), -1))
        grad_scores = weights * (grad_weights - delta_ref[head : head + 1, :])
        w_up, w_low = split_parts(weights)
        both = dot_plain(w_up, jnp.concatenate((do_up, do_low), -1))
        dv_ref[:, cols] += both[:, :HD] + both[:, HD:] + dot_plain(w_low, do_up)
        s_up, s_low = split_parts(grad_scores)
        both = dot_plain(s_up, jnp.concatenate((q_up, q_low), -1))
        dk_ref[:, cols] += both[:, :HD] + both[:, HD:] + dot_plain(s_low, q_up)
        both = dot_plain(kt_two[head], s_up)
        summed = both[:HD] + both[HD:] + dot_plain(kt_two[head, :HD], s_low)
        dq_ref[cols, :] = summed * HD ** (-0.5)


def whole(*dims):
    return pl.BlockSpec(dims, lambda step: (0,) * len(dims))


def query_block(count):
    for size in (256, 128):
        if count % size == 0:
            return size
    return count


def attend_forward(queries, keys_all, values_all, mask):
    count, columns = queries.shape
    key_count, heads = keys_all.shape[0], columns // HD
    block = query_block(count)
    return pl.pallas_call(
        functools.partial(attend_kernel, heads),
        grid=(count // block,),
        in_specs=[
            pl.BlockSpec((block, columns), lambda step: (step, 0)),
            whole(key_count, columns),
            whole(columns, key_count),
            whole(key_count, 1),
        ],
        out_specs=[
            pl.BlockSpec((columns, block), lambda step: (0, step)),
            pl.BlockSpec((heads, block), lambda step: (0, step)),
        ],
        out_shape=[
            jax.ShapeDtypeStruct((columns, count), jnp.float32),
            jax.ShapeDtypeStruct((heads, count), jnp.float32),
        ],
        scratch_shapes=[
            pltpu.VMEM((heads, key_count, 3 * HD), jnp.bfloat16),
            pltpu.VMEM((heads, 2 * HD, key_count), jnp.bfloat16),
        ],
        compiler_params=pltpu.CompilerParams(vmem_limit_bytes=48 * 2**20),
        cost_estimate=pl.CostEstimate(
            flops=12 * count * key_count * columns,
            bytes_accessed=16 * key_count * columns,
            transcendentals=count * key_count * heads,
        ),
    )(queries, keys_all, values_all.T, mask)


def attend_backward(queries, keys_all, values_all, mask, lse, delta, grad_attn):
    count, columns = queries.shape
    key_count, heads = keys_all.shape[0], columns // HD
    block = query_block(count)
    return pl.pallas_call(
        functools.partial(attend_back_kernel, heads),
        grid=(count // block,),
        in_specs=[
            pl.BlockSpec((block, columns), lambda step: (step, 0)),
            whole(key_count, columns),
            whole(key_count, columns),
            whole(columns, key_count),
            whole(key_count, 1),
            pl.BlockSpec((heads, block), lambda step: (0, step)),
            pl.BlockSpec((heads, block), lambda step: (0, step)),
            pl.BlockSpec((block, columns), lambda step: (step, 0)),
        ],
        out_specs=[
            pl.BlockSpec((columns, block), lambda step: (0, step)),
            whole(key_count, columns),
            whole(key_count, columns),
        ],
        out_shape=[
            jax.ShapeDtypeStruct((columns, count), jnp.float32),
            jax.ShapeDtypeStruct((key_count, columns), jnp.float32),
            jax.ShapeDtypeStruct((key_count, columns), jnp.float32),
        ],
        scratch_shapes=[
            pltpu.VMEM((heads, key_count, 3 * HD), jnp.bfloat16),
            pltpu.VMEM((heads, key_count, 3 * HD), jnp.bfloat16),
            pltpu.VMEM((heads, 2 * HD, key_count), jnp.bfloat16),
        ],
        compiler_params=pltpu.CompilerParams(vmem_limit_bytes=48 * 2**20),
        cost_estimate=pl.CostEstimate(
            flops=30 * count * key_count * columns,
            bytes_accessed=24 * key_count * columns,
            transcendentals=count * key_count * heads,
        ),
    )(queries, keys_all, values_all, keys_all.T, mask, lse, delta, grad_attn)


def owned_block(weight_block, dim_index, owned_count):
    return lax.dynamic_slice_in_dim(
        weight_block, lax.axis_index("dp") * owned_count, owned_count, dim_index
    )


def adamw(weight_old, gradient, first_old, second_old, decay_rate):
    first_new = beta_first * first_old + (1.0 - beta_first) * gradient
    second_new = beta_second * second_old + (1.0 - beta_second) * gradient * gradient
    step_dir = (
        first_new
        / (1.0 - beta_first**STEP)
        / (jnp.sqrt(second_new / (1.0 - beta_second**STEP)) + adam_epsilon)
    )
    return (first_new, second_new, weight_old - learn_rate * (step_dir + decay_rate * weight_old))


def local(
    frames,
    cotangent,
    w_qkv,
    w_out,
    w_up,
    w_down,
    vectors,
    first_qkv,
    second_qkv,
    first_out,
    second_out,
    first_up,
    second_up,
    first_down,
    second_down,
    first_vec,
    second_vec,
):
    frame_count, half_width = frames.shape[1:]
    width, columns = 2 * half_width, w_qkv.shape[2]
    local_heads = columns // HD
    core = lax.axis_index("gr")
    row_count = -(-frame_count // (2 * row_tile)) * row_tile
    chips = lax.axis_size("gc")
    count = chips * row_count

    vectors_all = lax.all_gather(vectors, "gr", axis=1, tiled=True)
    rows = own_rows(frames[0], row_count)
    normed, unit_one, scale_one = norm_forward(rows, vectors_all[0], vectors_all[1])
    normed_all = gather_tokens(normed)
    weights_qkv = in_core_order(w_qkv, other_core(w_qkv), 0).reshape(width, 3 * columns)
    weights_out = in_core_order(w_out, other_core(w_out), 1)
    weights_up = in_core_order(w_up, other_core(w_up), 0)
    weights_down = in_core_order(w_down, other_core(w_down), 1)
    grad_rows = own_rows(cotangent[0], row_count)
    grad_all = gather_tokens(grad_rows)

    mixed_qkv = product("td,dn->tn", normed_all, weights_qkv)
    queries = mixed_qkv[:, :columns]
    key_value = mixed_qkv[:, columns:]
    key_value_all = in_core_order(key_value, other_core(key_value), 0)
    keys_all, values_all = key_value_all[:, :columns], key_value_all[:, columns:]
    place = jnp.arange(2 * count)
    real = place // count * row_count + place % row_count < frame_count
    mask = jnp.where(real, 0.0, masked).astype(jnp.float32)[:, None]
    attended_t, lse = attend_forward(queries, keys_all, values_all, mask)

    middle = rows + scatter_tokens(product("nt,nd->td", attended_t, weights_out)) + vectors_all[2]
    normed_two, unit_two, scale_two = norm_forward(middle, vectors_all[3], vectors_all[4])
    normed_two_all = gather_tokens(normed_two)
    grad_active = product("td,fd->tf", grad_all, weights_down)
    hidden = product("td,df->tf", normed_two_all, weights_up)
    cumulative = 0.5 * (1.0 + lax.erf(hidden * 0.5**0.5))
    density = jnp.exp(-0.5 * hidden * hidden) * (0.5 / jnp.pi) ** 0.5
    active = hidden * cumulative
    grad_hidden = grad_active * (cumulative + hidden * density)
    grad_normed_two = scatter_tokens(product("tf,df->td", grad_hidden, weights_up))
    grad_middle_norm, grad_gain_two, grad_bias_two = norm_backward(
        grad_normed_two, unit_two, scale_two, vectors_all[3]
    )
    grad_middle = grad_rows + grad_middle_norm
    grad_middle_all = gather_tokens(grad_middle)

    block_rows = middle + scatter_tokens(product("tf,fd->td", active, weights_down)) + vectors_all[5]
    block_out = own_width(block_rows, frame_count)[None]
    grad_down = own_half_sum(product("tf,td->df", active, grad_all))
    grad_up = own_half_sum(product("td,tf->df", normed_two_all, grad_hidden))
    grad_out = own_half_sum(product("nt,td->dn", attended_t, grad_middle_all))

    grad_attn = product("td,nd->tn", grad_middle_all, weights_out)
    delta = jnp.sum((grad_attn.T * attended_t).reshape(local_heads, HD, count), 1)
    grad_queries_t, grad_keys, grad_values = attend_backward(
        queries, keys_all, values_all, mask, lse, delta, grad_attn
    )
    grad_pairs = jnp.concatenate((grad_keys, grad_values), 1)
    mine = lax.dynamic_slice_in_dim(grad_pairs, core * count, count, 0)
    sent = lax.dynamic_slice_in_dim(grad_pairs, (1 - core) * count, count, 0)
    grad_mixed = jnp.concatenate((grad_queries_t.T, mine + other_core(sent)), 1)
    grad_normed = scatter_tokens(product("tn,dn->td", grad_mixed, weights_qkv))
    grad_qkv = own_half_sum(product("td,tn->dn", normed_all, grad_mixed))
    grad_inputs, grad_gain_one, grad_bias_one = norm_backward(
        grad_normed, unit_one, scale_one, vectors_all[0]
    )
    grad_frames = own_width(grad_middle + grad_inputs, frame_count)[None]

    vector_local = jnp.stack(
        (
            grad_gain_one,
            grad_bias_one,
            jnp.sum(grad_middle, 0),
            grad_gain_two,
            grad_bias_two,
            jnp.sum(grad_rows, 0),
        )
    )
    grad_vectors = lax.psum(vector_local, ("dp", "gr", "gc"))
    grad_vectors = lax.dynamic_slice_in_dim(grad_vectors, core * half_width, half_width, 1)
    grad_down, grad_up, grad_out, grad_qkv = (
        lax.psum_scatter(part, "dp", scatter_dimension=0, tiled=True)
        for part in (grad_down, grad_up, grad_out, grad_qkv)
    )
    grad_down, grad_out = grad_down.T, grad_out.T
    grad_qkv = grad_qkv.reshape(grad_qkv.shape[0], 3, columns)
    first_qkv_new, second_qkv_new, w_qkv_new = adamw(
        owned_block(w_qkv, 0, grad_qkv.shape[0]), grad_qkv, first_qkv, second_qkv, weight_decay
    )
    first_out_new, second_out_new, w_out_new = adamw(
        owned_block(w_out, 1, grad_out.shape[1]), grad_out, first_out, second_out, weight_decay
    )
    first_up_new, second_up_new, w_up_new = adamw(
        owned_block(w_up, 0, grad_up.shape[0]), grad_up, first_up, second_up, weight_decay
    )
    first_down_new, second_down_new, w_down_new = adamw(
        owned_block(w_down, 1, grad_down.shape[1]), grad_down, first_down, second_down, weight_decay
    )
    first_vec_new, second_vec_new, vectors_new = adamw(
        vectors, grad_vectors, first_vec, second_vec, 0.0
    )
    return (
        block_out,
        grad_frames,
        grad_qkv,
        first_qkv_new,
        second_qkv_new,
        w_qkv_new,
        grad_out,
        first_out_new,
        second_out_new,
        w_out_new,
        grad_up,
        first_up_new,
        second_up_new,
        w_up_new,
        grad_down,
        first_down_new,
        second_down_new,
        w_down_new,
        grad_vectors,
        first_vec_new,
        second_vec_new,
        vectors_new,
    )


def solution(mesh):
    return jax.shard_map(
        local,
        mesh=mesh,
        in_specs=(
            P("dp", "gc", "gr"),
            P("dp", "gc", "gr"),
            P("gr", None, "gc"),
            P("gc", "gr"),
            P("gr", "gc"),
            P("gc", "gr"),
            P(None, "gr"),
            P(("gr", "dp"), None, "gc"),
            P(("gr", "dp"), None, "gc"),
            P("gc", ("gr", "dp")),
            P("gc", ("gr", "dp")),
            P(("gr", "dp"), "gc"),
            P(("gr", "dp"), "gc"),
            P("gc", ("gr", "dp")),
            P("gc", ("gr", "dp")),
            P(None, "gr"),
            P(None, "gr"),
        ),
        out_specs=(
            P("dp", "gc", "gr"),
            P("dp", "gc", "gr"),
            P(("gr", "dp"), None, "gc"),
            P(("gr", "dp"), None, "gc"),
            P(("gr", "dp"), None, "gc"),
            P(("gr", "dp"), None, "gc"),
            P("gc", ("gr", "dp")),
            P("gc", ("gr", "dp")),
            P("gc", ("gr", "dp")),
            P("gc", ("gr", "dp")),
            P(("gr", "dp"), "gc"),
            P(("gr", "dp"), "gc"),
            P(("gr", "dp"), "gc"),
            P(("gr", "dp"), "gc"),
            P("gc", ("gr", "dp")),
            P("gc", ("gr", "dp")),
            P("gc", ("gr", "dp")),
            P("gc", ("gr", "dp")),
            P(None, "gr"),
            P(None, "gr"),
            P(None, "gr"),
            P(None, "gr"),
        ),
        check_vma=False,
    )
```

time: 1240 us -> 643 us (0.52)
  waiting for transfers between devices: 680 us -> 400 us
  matrix products: 198 us -> 58.2 us
  local copies, waits for them, and re-layouts: 143 us -> 42 us
  other arithmetic: 103 us -> 42.8 us
  blocking collectives: 85.6 us -> 42 us
  Pallas kernels: 0 us -> 28.7 us
    unnamed x29 -> x14, waiting for transfers between devices: 458 us -> 50.9 us
    reduce_scatter x3 -> x6, waiting for transfers between devices: 29.4 us -> 183 us  [the longest x4 183 us: scatter_tokens(): lax.psum_scatter(partial_value, 'gc', scatter_dimension=0, tiled=True)]
    dot_general x16 -> x12, matrix products: 183 us -> 58.2 us  [product(): return jnp.einsum(spec, left, right, precision=high)]
    dot_general x6 -> x1, local copies, waits for them, and re-layouts: 84.3 us -> 1.2 us  [product(): return jnp.einsum(spec, left, right, precision=high)]
    psum x5 -> x1, blocking collectives: 85.6 us -> 39.9 us  [local(): grad_vectors = lax.psum(vector_local, ('dp', 'gr', 'gc'))]
    add_any x1 -> x0, other arithmetic: 44.8 us -> none  [gelu_exact(): return jax.nn.gelu(inputs, approximate=False)]
    all_gather x10 -> x4, waiting for transfers between devices: 193 us -> 156 us  [gather_tokens(): return lax.all_gather(rows, 'gc', axis=0, tiled=True)]
    pallas_call x0 -> x2, Pallas kernels: none -> 28.7 us  [the longest x1 19.7 us: attend_backward(): pl.pallas_call(functools.partial(attend_back_kernel, heads), grid=(count...]
  transfers between devices with their start and end apart: 21 -> 26, of which waited for: 15 -> 15; matrix products, arithmetic and copies ran while one was open for 17% -> 15% of each run, Pallas kernels for 0% -> 3%
where the time goes in v1:
time: 643 us; the launch traced here: 634 us
  waiting for transfers between devices  400 us (62%)
  matrix products  58.2 us (9%)
  other arithmetic  42.8 us (7%)
  local copies, waits for them, and re-layouts  42 us (7%)
  blocking collectives  42 us (7%)
  Pallas kernels  28.7 us (4%)
  between operations  15.6 us (2%)
    reduce_scatter x4, waiting for transfers between devices, scatter_tokens(): lax.psum_scatter(partial_value, 'gc', scatter_dimension=0, tiled=True)  183 us
    all_gather x4, waiting for transfers between devices, gather_tokens(): return lax.all_gather(rows, 'gc', axis=0, tiled=True)  156 us
    dot_general x12, matrix products, product(): return jnp.einsum(spec, left, right, precision=high)  58.2 us
    unnamed x14, waiting for transfers between devices  50.9 us
    psum x1, blocking collectives, local(): grad_vectors = lax.psum(vector_local, ('dp', 'gr', 'gc'))  39.9 us
    unnamed x132, local copies, waits for them, and re-layouts  29.8 us
    pallas_call x1, Pallas kernels, attend_backward(): pl.pallas_call(functools.partial(attend_back_kernel, heads), grid=(count...  19.7 us
  transfers between devices with their start and end apart: 26, of which 15 were waited for; matrix products, arithmetic and copies ran while one was open for 15% of the time, Pallas kernels for 3%

profile of v1, /device:TPU:0, one launch (start us, length us, event | category | flops | bytes accessed | tf_op | source)
XLA Modules:
  0.0 633.9 jit_solution(4423114645292511057)
XLA Ops:
  16.4 50.2 %all-gather.5.cloned.1.call-done = f32[768,768]{1,0:T(8,128)} async-done(((f32[192,768]{1,0:T(8,128)}), f32[768,768]{1,0:T(8,128)}) %all-gather.5.cloned.1.call-update) | async-done | bytes 2359312 | tf_op jit(solution)/shard_map/all_gather | solution.py:31
  66.7 3.9 fusion.63
  82.8 9.0 %shard_map.336 = (f32[192,768]{1,0:T(8,128)S(1)}, f32[3,768]{1,0:T(4,128)S(1)}) custom-call(f32[768,192]{1,0:T(8,128)S(1)} %copy-done.3, f32[1536,192]{1,0:T(8,128)S(1)} %copy-done, f32[192,1536]{1,0:T(8,128)S(1)} %bitcast.39, f32[1536,1]{1,0:T(8,128)S(1)} %copy-done.1), custom_call_target="tpu_custom_call" | custom-call | flops 2717908992 | bytes 4718592 | tf_op jit(solution)/shard_map/pallas_call | solution.py:182
  94.6 47.0 %reduce-scatter.13.cloned.1.call-done = f32[192,768]{1,0:T(8,128)} async-done(((f32[768,768]{1,0:T(8,128)}), f32[192,768]{1,0:T(8,128)}) %reduce-scatter.13.cloned.1.call-update) | async-done | bytes 589840 | tf_op jit(solution)/shard_map/reduce_scatter | solution.py:35
  153.9 3.3 broadcast_select_fusion.1
  158.8 36.8 %all-gather.7.cloned.1.call-done = f32[768,768]{1,0:T(8,128)} async-done(((f32[192,768]{1,0:T(8,128)}), f32[768,768]{1,0:T(8,128)}) %all-gather.7.cloned.1.call-update) | async-done | bytes 2359312 | tf_op jit(solution)/shard_map/all_gather | solution.py:31
  195.6 6.8 %fusion.8 = f32[768,768]{1,0:T(8,128)} fusion(f32[768,768]{1,0:T(8,128)} %all-gather.7.cloned.1.call-done, f32[384,768]{1,0:T(8,128)} %get-tuple-element.117, f32[384,768]{1,0:T(8,128)} %get-tuple-element.116), kind=kOutput, calls=%fused_computation.23 | convolution fusion | flops 2718498816 | bytes 7077888 | tf_op jit(solution)/shard_map/td,df->tf/dot_general | solution.py:27
  202.4 44.0 %all-gather.9.cloned.1.call-done = f32[768,768]{1,0:T(8,128)} async-done(((f32[192,768]{1,0:T(8,128)}), f32[768,768]{1,0:T(8,128)}) %all-gather.9.cloned.1.call-update) | async-done | bytes 2359312 | tf_op jit(solution)/shard_map/all_gather | solution.py:31
  246.4 6.8 %fusion.4 = f32[768,768]{1,0:T(8,128)S(1)} fusion(f32[768,768]{1,0:T(8,128)} %fusion.8, f32[768,768]{1,0:T(8,128)} %all-gather.9.cloned.1.call-done, f32[768,384]{0,1:T(8,128)} %get-tuple-element.119, f32[768,384]{0,1:T(8,128)} %get-tuple-element.118), kind=kOutput, calls=%fused_computation.9 | convolution fusion | flops 2723807232 | bytes 9437184 | tf_op jit(solution)/shard_map/td,fd->tf/dot_general | solution.py:27
  254.5 4.5 fusion.7
  259.3 7.0 %fusion.6 = f32[768,768]{1,0:T(8,128)} fusion(f32[768,384]{0,1:T(8,128)} %get-tuple-element.119, f32[768,384]{0,1:T(8,128)} %get-tuple-element.118, f32[768,768]{1,0:T(8,128)} %fusion.8), kind=kOutput, calls=%fused_computation.21 | convolution fusion | flops 2720858112 | bytes 7077888 | tf_op jit(solution)/shard_map/tf,fd->td/dot_general | solution.py:27
  266.4 39.7 %reduce-scatter.17.cloned.1.call-done = f32[192,768]{1,0:T(8,128)} async-done(((f32[768,768]{1,0:T(8,128)}), f32[192,768]{1,0:T(8,128)}) %reduce-scatter.17.cloned.1.call-update) | async-done | bytes 589840 | tf_op jit(solution)/shard_map/reduce_scatter | solution.py:35
  308.7 47.1 %reduce-scatter.15.cloned.1.call-done = f32[192,768]{1,0:T(8,128)} async-done(((f32[768,768]{1,0:T(8,128)}), f32[192,768]{1,0:T(8,128)}) %reduce-scatter.15.cloned.1.call-update) | async-done | bytes 589840 | tf_op jit(solution)/shard_map/reduce_scatter | solution.py:35
  355.8 3.4 fusion.53
  359.3 5.9 fusion.19
  374.0 6.0 fusion.65
  384.3 25.1 %all-gather.11.cloned.1.call-done = f32[768,768]{1,0:T(8,128)} async-done(((f32[192,768]{1,0:T(8,128)}), f32[768,768]{1,0:T(8,128)}) %all-gather.11.cloned.1.call-update) | async-done | bytes 2359312 | tf_op jit(solution)/shard_map/all_gather | solution.py:31
  417.1 19.7 %shard_map.337 = (f32[192,768]{1,0:T(8,128)S(1)}, f32[1536,192]{1,0:T(8,128)S(1)}, f32[1536,192]{1,0:T(8,128)}) custom-call(f32[768,192]{1,0:T(8,128)S(1)} %copy-done.4, f32[1536,192]{1,0:T(8,128)} %copy.57.k_ref, f32[1536,192]{1,0:T(8,128)} %copy.62.v_ref, f32[192,1536]{1,0:T(8,128)S(1)} %bitcast.38, f32[1536,1]{1,0:T(8,128)S(1)} %copy-done.2, ...), custom_call_target="tpu_custom_call" | custom-call | flops 6794772480 | bytes 7077888 | tf_op jit(solution)/shard_map/pallas_call | solution.py:216
  448.9 3.2 fusion.13
  463.1 5.6 fusion.14
  476.7 23.2 %reduce-scatter.27.cloned.1.call-done = f32[96,192]{1,0:T(8,128)} async-done(((f32[384,192]{1,0:T(8,128)}), f32[96,192]{1,0:T(8,128)}) %reduce-scatter.27.cloned.1.call-update) | async-done | bytes 73744
  502.7 27.5 %reduce-scatter.25.cloned.1.call-done = f32[96,576]{1,0:T(8,128)} async-done(((f32[384,576]{1,0:T(8,128)}), f32[96,576]{1,0:T(8,128)}) %reduce-scatter.25.cloned.1.call-update) | async-done | bytes 221200
  531.5 48.9 %reduce-scatter.19.cloned.1.call-done = f32[192,768]{1,0:T(8,128)} async-done(((f32[768,768]{1,0:T(8,128)}), f32[192,768]{1,0:T(8,128)}) %reduce-scatter.19.cloned.1.call-update) | async-done | bytes 589840 | tf_op jit(solution)/shard_map/reduce_scatter | solution.py:35
  584.5 39.9 %psum.7 = f32[6,768]{1,0:T(8,128)S(1)} all-reduce(f32[6,768]{1,0:T(8,128)S(1)} %stack.27), channel_id=1, replica_groups=mesh['dp'=4,'gr'=2,'gc'=4] {'dp','gr','gc'}, use_global_device_ids=true, to_apply=%region_24.25 | all-reduce | flops 4608 | bytes 36864 | tf_op jit(solution)/shard_map/psum | solution.py:366
  (254 shorter events, 103.6 us)
Async XLA Ops:
  7.2 59.5 %all-gather.5.cloned.1.call-start = ((), (), s32[]{:S(2)}) async-start(), calls=%async_computation.8 | async-start | bytes 2949120 | tf_op jit(solution)/shard_map/all_gather | solution.py:31
  8.4 3.2 collective-permute-start
  13.6 128.0 %reduce-scatter.13.cloned.1.call-start = ((), (), s32[]{:S(2)}) async-start(), calls=%async_computation.9 | async-start | bytes 2949120 | tf_op jit(solution)/shard_map/reduce_scatter | solution.py:35
  13.6 2.5 collective-permute-start.1
  71.7 4.2 collective-permute-start.2
  71.7 2.9 collective-permute-start.3
  94.6 101.1 %all-gather.7.cloned.1.call-start = ((), (), s32[]{:S(2)}) async-start(), calls=%async_computation.10 | async-start | bytes 2949120 | tf_op jit(solution)/shard_map/all_gather | solution.py:31
  145.5 100.9 %all-gather.9.cloned.1.call-start = ((), (), s32[]{:S(2)}) async-start(), calls=%async_computation.12 | async-start | bytes 2949120 | tf_op jit(solution)/shard_map/all_gather | solution.py:31
  150.1 156.0 %reduce-scatter.17.cloned.1.call-start = ((), (), s32[]{:S(2)}) async-start(), calls=%async_computation.13 | async-start | bytes 2949120 | tf_op jit(solution)/shard_map/reduce_scatter | solution.py:35
  150.6 3.3 collective-permute-start.4
  153.6 3.6 collective-permute-start.5
  259.1 96.7 %reduce-scatter.15.cloned.1.call-start = ((), (), s32[]{:S(2)}) async-start(), calls=%async_computation.11 | async-start | bytes 2949120 | tf_op jit(solution)/shard_map/reduce_scatter | solution.py:35
  266.3 143.1 %all-gather.11.cloned.1.call-start = ((), (), s32[]{:S(2)}) async-start(), calls=%async_computation.14 | async-start | bytes 2949120 | tf_op jit(solution)/shard_map/all_gather | solution.py:31
  359.3 111.6 %reduce-scatter.23.cloned.1.call-start = ((), (), s32[]{:S(2)}) async-start(), calls=%async_computation.17 | async-start | bytes 1474560 | tf_op jit(solution)/shard_map/reduce_scatter | solution.py:369
  367.9 3.2 collective-permute-start.13
  374.0 99.0 %reduce-scatter.21.cloned.1.call-start = ((), (), s32[]{:S(2)}) async-start(), calls=%async_computation.16 | async-start | bytes 1474560 | tf_op jit(solution)/shard_map/reduce_scatter | solution.py:369
  382.5 57.7 %collective-permute-start.12 = (f32[384,768]{1,0:T(8,128)}, f32[384,768]{1,0:T(8,128)}, u32[]{:S(2)}, u32[]{:S(2)}) collective-permute-start(f32[384,768]{1,0:T(8,128)} %constant_dynamic-slice_fusion.2), channel_id=1, source_target_pairs={{0,4},{4,0},{1,5},{5,1},{2,6},{6,2},{3,7},{7,3},{8,12},{12,8},{9,1... | collective-permute-start | bytes 3538952 | tf_op jit(solution)/shard_map/ppermute | solution.py:39
  440.2 6.5 %collective-permute-start.8 = (f32[768,384]{1,0:T(8,128)}, f32[768,384]{1,0:T(8,128)}, u32[]{:S(2)}, u32[]{:S(2)}) collective-permute-start(f32[768,384]{1,0:T(8,128)} %fusion.16), channel_id=1, source_target_pairs={{0,4},{4,0},{1,5},{5,1},{2,6},{6,2},{3,7},{7,3},{8,12},{12,8},{9,1... | collective-permute-start | bytes 3538952 | tf_op jit(solution)/shard_map/ppermute | solution.py:39
  442.8 57.2 %reduce-scatter.27.cloned.1.call-start = ((), (), s32[]{:S(2)}) async-start(), calls=%async_computation.19 | async-start | bytes 491520
  453.7 4.2 collective-permute-start.10
  457.6 72.7 %reduce-scatter.25.cloned.1.call-start = ((), (), s32[]{:S(2)}) async-start(), calls=%async_computation.18 | async-start | bytes 1228800
  463.1 117.4 %reduce-scatter.19.cloned.1.call-start = ((), (), s32[]{:S(2)}) async-start(), calls=%async_computation.15 | async-start | bytes 2949120 | tf_op jit(solution)/shard_map/reduce_scatter | solution.py:35
  470.4 4.8 collective-permute-start.6
  583.3 41.8 %collective-permute-start.9 = (f32[192,384]{1,0:T(8,128)S(1)}, f32[192,384]{1,0:T(8,128)S(1)}, u32[]{:S(2)}, u32[]{:S(2)}) collective-permute-start(f32[192,384]{1,0:T(8,128)S(1)} %constant_dynamic-slice_fusion.6), channel_id=1, source_target_pairs={{0,4},{4,0},{1,5},{5,1},{2,6},{6,2},{3,7},{7,3},{8,12},{12,8},{9,1... | collective-permute-start | bytes 884744 | tf_op jit(solution)/shard_map/ppermute | solution.py:39
  (62 other events, 1208.0 us)
Sparse Core Ops, SparseCore 0:
  13.7 52.9 all-gather.4
  94.7 46.8 reduce-scatter.12
  145.6 49.9 all-gather.6
  197.0 49.2 all-gather.8
  259.2 46.8 reduce-scatter.16
  308.3 47.5 reduce-scatter.14
  359.4 49.9 all-gather.10
  412.9 27.3 reduce-scatter.22
  443.8 28.5 reduce-scatter.20
  475.6 24.3 reduce-scatter.26
  502.9 27.2 reduce-scatter.24
  532.4 48.0 reduce-scatter.18
